TPU v7x, 256 devices: a whole 4x4x8 slice. The times are simulated.
256 devices in a mesh: pipe: 16 (over x_lo, y, core), expert: 8 (over z), dp: 2 (over x_hi).
Axes of the slice: x: 4 (x_hi: 2, x_lo: 2; x = x_hi * 2 + x_lo), y: 4, z: 8, core: 2. Of those that a mesh axis runs over, the one named last changes fastest.
Arguments:
- fwd_in: bfloat16 [16, 2048, 3584], P('pipe', ('expert', 'dp')), may hold values from -6 to 6
- fwd_ids: int32 [16, 2048, 1], P('pipe', ('expert', 'dp')), may hold values from 0 to 3; in each aligned block of 128 rows (0 to 127, 128 to 255, ..., all dimensions but the last counted through in order) at most 40 rows name the same one
- fwd_gates: float32 [16, 2048, 1], P('pipe', ('expert', 'dp')), may hold values from 0.2 to 1
- bwd_in: bfloat16 [16, 2048, 3584], P('pipe', ('expert', 'dp')), may hold values from -6 to 6
- bwd_grad: bfloat16 [16, 2048, 3584], P('pipe', ('expert', 'dp')), may hold values from -6 to 6
- bwd_ids: int32 [16, 2048, 1], P('pipe', ('expert', 'dp')), may hold values from 0 to 3; in each aligned block of 128 rows (0 to 127, 128 to 255, ..., all dimensions but the last counted through in order) at most 40 rows name the same one
- bwd_gates: float32 [16, 2048, 1], P('pipe', ('expert', 'dp')), may hold values from 0.2 to 1
- gate_w: bfloat16 [16, 3584, 4096], P('pipe', 'dp', 'expert'), may hold values from -0.09375 to 0.09375
- up_w: bfloat16 [16, 3584, 4096], P('pipe', 'dp', 'expert'), may hold values from -0.09375 to 0.09375
- down_w: bfloat16 [16, 3584, 4096], P('pipe', 'dp', 'expert'), may hold values from -0.1875 to 0.1875
Outputs:
- fwd_next: bfloat16 [16, 2048, 3584], P('pipe', ('expert', 'dp'))
- bwd_next: bfloat16 [16, 2048, 3584], P('pipe', ('expert', 'dp'))
- gate_grad: bfloat16 [16, 3584, 4096], P('pipe', 'dp', 'expert')
Inputs may be any that keep to these rules, and one draw needn't show every extreme that they name: `fwd_ids`: at every section the 128 tokens of one routing block (aligned blocks of rows) name any expert at most 40 times, a bound that some block reaches; each token names exactly 1 expert. `bwd_ids`: as for fwd_ids.
All inputs are finite; a program needn't handle non-finite values.
Results may differ from a plain program's by a relative error of at most 0.01.
Values may be sent and summed in bfloat16 or wider, within the bound.
A program may use at most 128 MiB of HBM per device.

v0:
```python
import jax
import jax.numpy as jnp
from jax import lax
from jax.sharding import PartitionSpec as P

SPLIT = 2


def shifted(block, axis, distance):
    devices = range(lax.axis_size(axis))
    route = [((i - distance) % len(devices), i) for i in devices]
    return lax.ppermute(block, axis, route)


def slot_index(ids, experts, capacity):
    flat = ids.reshape(-1)
    onehot = (flat[:, None] == jnp.arange(experts, dtype=jnp.int32)[None, :]).astype(jnp.int32)
    ranked = jnp.sum(onehot * (jnp.cumsum(onehot, axis=0) - 1), axis=1)
    return flat * capacity + ranked


def dispatch(rows, index, experts, capacity):
    empty = jnp.zeros((experts * capacity, rows.shape[1]), rows.dtype)
    placed = empty.at[index].set(rows).reshape(experts, capacity, rows.shape[1])
    return jnp.repeat(placed, SPLIT, axis=0)


def merge_halves(returned, experts):
    shape = returned.shape
    parts = returned.reshape(experts, SPLIT, shape[1], shape[2]).astype(jnp.float32)
    return jnp.sum(parts, axis=1)


def collect(output, index, gates, base):
    picked = output.reshape(-1, output.shape[2])[index].reshape(gates.shape[0], gates.shape[1], -1)
    total = base.astype(jnp.float32) + jnp.sum(gates[:, :, None] * picked, axis=1)
    return total.astype(jnp.bfloat16)


def expert_forward(received, w_gate, w_up, w_down):
    shape = received.shape
    rows = received.reshape(-1, shape[2])
    gate_pre = jnp.dot(rows, w_gate, preferred_element_type=jnp.float32)
    up_pre = jnp.dot(rows, w_up, preferred_element_type=jnp.float32)
    hidden = (jax.nn.silu(gate_pre) * up_pre).astype(jnp.bfloat16)
    output = lax.dot_general(
        hidden, w_down, (((1,), (1,)), ((), ())), preferred_element_type=jnp.float32
    )
    return output.astype(jnp.bfloat16).reshape(shape)


def expert_backward(x_recv, z_recv, w_gate, w_up, w_down):
    shape = x_recv.shape
    x_rows = x_recv.reshape(-1, shape[2])
    z_rows = z_recv.reshape(-1, shape[2])
    gate_pre = jnp.dot(x_rows, w_gate, preferred_element_type=jnp.float32)
    up_pre = jnp.dot(x_rows, w_up, preferred_element_type=jnp.float32)
    sigma = jax.nn.sigmoid(gate_pre)
    active = gate_pre * sigma
    d_hidden = jnp.dot(z_rows, w_down, preferred_element_type=jnp.float32)
    d_gate = (d_hidden * up_pre * sigma * (1.0 + gate_pre * (1.0 - sigma))).astype(jnp.bfloat16)
    d_up = (d_hidden * active).astype(jnp.bfloat16)
    contract = (((1,), (1,)), ((), ()))
    back = lax.dot_general(d_gate, w_gate, contract, preferred_element_type=jnp.float32)
    back = back + lax.dot_general(d_up, w_up, contract, preferred_element_type=jnp.float32)
    inner = (shape[0], shape[1], w_gate.shape[1])
    return (back.astype(jnp.bfloat16).reshape(shape), d_gate.reshape(inner))


def per_device(
    fwd_in, fwd_ids, fwd_gates, bwd_in, bwd_grad, bwd_ids, bwd_gates, gate_w, up_w, down_w
):
    holders = lax.axis_size("expert")
    experts = holders // SPLIT
    w_gate, w_up, w_down = (
        lax.all_gather(gate_w[0], "dp", axis=0, tiled=True),
        lax.all_gather(up_w[0], "dp", axis=0, tiled=True),
        lax.all_gather(down_w[0], "dp", axis=0, tiled=True),
    )
    f_rows = fwd_in[0]
    x_rows_in = bwd_in[0]
    g_rows = bwd_grad[0]
    row_count = f_rows.shape[0]
    features = f_rows.shape[1]
    picks = fwd_ids.shape[2]
    capacity = min(row_count, row_count * picks * 5 // (4 * experts))
    f_index = slot_index(fwd_ids[0], experts, capacity)
    f_buf = dispatch(jnp.repeat(f_rows, picks, axis=0), f_index, experts, capacity)
    b_index = slot_index(bwd_ids[0], experts, capacity)
    scaled = (bwd_gates[0][:, :, None] * g_rows[:, None, :].astype(jnp.float32)).astype(
        jnp.bfloat16
    )
    x_buf = dispatch(jnp.repeat(x_rows_in, picks, axis=0), b_index, experts, capacity)
    z_buf = dispatch(scaled.reshape(-1, features), b_index, experts, capacity)
    received = lax.all_to_all(f_buf, "expert", split_axis=0, concat_axis=0, tiled=True)
    f_back = lax.all_to_all(
        expert_forward(received, w_gate, w_up, w_down),
        "expert",
        split_axis=0,
        concat_axis=0,
        tiled=True,
    )
    x_recv, z_recv = (
        lax.all_to_all(x_buf, "expert", split_axis=0, concat_axis=0, tiled=True),
        lax.all_to_all(z_buf, "expert", split_axis=0, concat_axis=0, tiled=True),
    )
    back, d_gate = expert_backward(x_recv, z_recv, w_gate, w_up, w_down)
    b_back = lax.all_to_all(back, "expert", split_axis=0, concat_axis=0, tiled=True)
    layer_out = collect(merge_halves(f_back, experts), f_index, fwd_gates[0], f_rows)
    input_grad = collect(
        merge_halves(b_back, experts), b_index, jnp.ones_like(bwd_gates[0]), g_rows
    )
    fwd_next = shifted(layer_out[None], "pipe", 1)
    bwd_next = shifted(input_grad[None], "pipe", -1)
    hidden_units = w_gate.shape[1]
    x_rows = x_recv.reshape(-1, features)
    gate_rows = d_gate.reshape(-1, hidden_units)
    contract = (((0,), (0,)), ((), ()))
    summed = lax.psum_scatter(
        lax.dot_general(x_rows, gate_rows, contract, preferred_element_type=jnp.float32).astype(
            jnp.bfloat16
        ),
        "dp",
        scatter_dimension=0,
        tiled=True,
    )
    gate_grad = summed[None]
    return (fwd_next, bwd_next, gate_grad)


def solution(mesh):
    return jax.shard_map(
        per_device,
        mesh=mesh,
        in_specs=(
            P("pipe", ("expert", "dp"), None),
            P("pipe", ("expert", "dp"), None),
            P("pipe", ("expert", "dp"), None),
            P("pipe", ("expert", "dp"), None),
            P("pipe", ("expert", "dp"), None),
            P("pipe", ("expert", "dp"), None),
            P("pipe", ("expert", "dp"), None),
            P("pipe", "dp", "expert"),
            P("pipe", "dp", "expert"),
            P("pipe", "dp", "expert"),
        ),
        out_specs=(
            P("pipe", ("expert", "dp"), None),
            P("pipe", ("expert", "dp"), None),
            P("pipe", "dp", "expert"),
        ),
        check_vma=False,
    )
```

profile of v0, /device:TPU:33, one launch (start us, length us, event | category | flops | bytes accessed | tf_op | source)
XLA Modules:
  0.0 346.1 jit_solution(5725379315154069737)
XLA Ops:
  14.2 8.1 %all-to-all-start = ((bf16[8,40,3584]{2,1,0:T(8,128)(2,1)}), bf16[8,40,3584]{2,1,0:T(8,128)(2,1)}, u32[]{:S(2)}, u32[]{:S(2)}) async-start(bf16[8,40,3584]{2,1,0:T(8,128)(2,1)} %bitcast.7), calls=%async_computation | async-start | bytes 4587520 | tf_op jit(solution)/shard_map/all_to_all | solution.py:95
  25.8 50.0 %all-to-all-done = bf16[8,40,3584]{2,1,0:T(8,128)(2,1)} async-done(((bf16[8,40,3584]{2,1,0:T(8,128)(2,1)}), bf16[8,40,3584]{2,1,0:T(8,128)(2,1)}, u32[]{:S(2)}, u32[]{:S(2)}) %all-to-all-start) | async-done | bytes 2293792 | tf_op jit(solution)/shard_map/all_to_all | solution.py:95
  77.4 4.3 %all-to-all-start.2 = ((bf16[8,40,3584]{2,1,0:T(8,128)(2,1)}), bf16[8,40,3584]{2,1,0:T(8,128)(2,1)}, u32[]{:S(2)}, u32[]{:S(2)}) async-start(bf16[8,40,3584]{2,1,0:T(8,128)(2,1)} %bitcast.23), calls=%async_computation.2 | async-start | bytes 4587520 | tf_op jit(solution)/shard_map/all_to_all | solution.py:105
  84.7 45.0 %all-to-all-done.2 = bf16[8,40,3584]{2,1,0:T(8,128)(2,1)} async-done(((bf16[8,40,3584]{2,1,0:T(8,128)(2,1)}), bf16[8,40,3584]{2,1,0:T(8,128)(2,1)}, u32[]{:S(2)}, u32[]{:S(2)}) %all-to-all-start.2) | async-done | bytes 2293792 | tf_op jit(solution)/shard_map/all_to_all | solution.py:105
  131.2 8.6 %all-to-all-start.3 = ((bf16[8,40,3584]{2,1,0:T(8,128)(2,1)}), bf16[8,40,3584]{2,1,0:T(8,128)(2,1)S(1)}, u32[]{:S(2)}, u32[]{:S(2)}) async-start(bf16[8,40,3584]{2,1,0:T(8,128)(2,1)} %bitcast.27), calls=%async_computation.3 | async-start | bytes 4587520 | tf_op jit(solution)/shard_map/all_to_all | solution.py:104
  139.8 4.5 %fusion.13 = f32[320,512]{1,0:T(8,128)S(1)} fusion(bf16[320,3584]{1,0:T(8,128)(2,1)} %bitcast.8, bf16[1,3584,512]{2,1,0:T(8,128)(2,1)} %all-gather.7.cloned.1.call-done), kind=kOutput, calls=%fused_computation.23 | convolution fusion | flops 1174405120 | bytes 6619136 | tf_op jit(solution)/shard_map/dot_general | solution.py:43
  144.3 43.1 %all-gather.9.cloned.1.call-done = bf16[1,3584,512]{2,1,0:T(8,128)(2,1)} async-done(((bf16[1,1792,512]{2,1,0:T(8,128)(2,1)}), bf16[1,3584,512]{2,1,0:T(8,128)(2,1)}) %all-gather.9.cloned.1.call-update) | async-done | bytes 3670032 | tf_op jit(solution)/shard_map/all_gather | solution.py:77
  187.4 7.9 %convolution_convert_fusion.1 = bf16[320,3584]{1,0:T(8,128)(2,1)} fusion(bf16[1,3584,512]{2,1,0:T(8,128)(2,1)} %all-gather.11.cloned.1.call-done, bf16[320,3584]{1,0:T(8,128)(2,1)} %bitcast.8, bf16[1,3584,512]{2,1,0:T(8,128)(2,1)} %all-gather.9.cloned.1.call-done, f32[320,512]{1,0:T(8,128)S(1)} %fusion.13), kind=kOutput, calls=%fused_computation.8 | convolution fusion | flops 2350940160 | bytes 12582912 | tf_op jit(solution)/shard_map/dot_general | solution.py:46
  196.7 6.9 %all-to-all-start.1 = ((bf16[8,40,3584]{2,1,0:T(8,128)(2,1)}), bf16[8,40,3584]{2,1,0:T(8,128)(2,1)S(1)}, u32[]{:S(2)}, u32[]{:S(2)}) async-start(bf16[8,40,3584]{2,1,0:T(8,128)(2,1)} %bitcast.107), calls=%async_computation.1 | async-start | bytes 4587520 | tf_op jit(solution)/shard_map/all_to_all | solution.py:96
  203.7 4.2 %fusion.1 = f32[320,512]{1,0:T(8,128)S(1)} fusion(bf16[320,3584]{1,0:T(8,128)(2,1)} %bitcast.24, bf16[1,3584,512]{2,1,0:T(8,128)(2,1)} %all-gather.11.cloned.1.call-done), kind=kOutput, calls=%fused_computation.11 | convolution fusion | flops 1174405120 | bytes 6619136 | tf_op jit(solution)/shard_map/dot_general | solution.py:60
  211.7 4.0 %convolution_convert_fusion = bf16[3584,512]{1,0:T(8,128)(2,1)} fusion(bf16[320,3584]{1,0:T(8,128)(2,1)S(1)} %bitcast.110, bf16[320,512]{1,0:T(8,128)(2,1)S(1)} %fusion.32), kind=kOutput, calls=%fused_computation.5 | convolution fusion | flops 1176240128 | bytes 6291456 | tf_op jit(solution)/shard_map/dot_general | solution.py:120
  215.7 3.6 %fusion.9 = f32[320,3584]{1,0:T(8,128)S(1)} fusion(bf16[320,512]{1,0:T(8,128)(2,1)S(1)} %fusion.32, bf16[1,3584,512]{2,1,0:T(8,128)(2,1)} %all-gather.7.cloned.1.call-done), kind=kOutput, calls=%fused_computation.19 | convolution fusion | flops 1174405120 | bytes 8585216 | tf_op jit(solution)/shard_map/dot_general | solution.py:64
  219.3 2.8 fusion
  222.1 34.9 %all-to-all-done.1 = bf16[8,40,3584]{2,1,0:T(8,128)(2,1)S(1)} async-done(((bf16[8,40,3584]{2,1,0:T(8,128)(2,1)}), bf16[8,40,3584]{2,1,0:T(8,128)(2,1)S(1)}, u32[]{:S(2)}, u32[]{:S(2)}) %all-to-all-start.1) | async-done | bytes 2293792 | tf_op jit(solution)/shard_map/all_to_all | solution.py:96
  258.3 4.3 %all-to-all-start.4 = ((bf16[8,40,3584]{2,1,0:T(8,128)(2,1)}), bf16[8,40,3584]{2,1,0:T(8,128)(2,1)}, u32[]{:S(2)}, u32[]{:S(2)}) async-start(bf16[8,40,3584]{2,1,0:T(8,128)(2,1)} %bitcast.29), calls=%async_computation.4 | async-start | bytes 4587520 | tf_op jit(solution)/shard_map/all_to_all | solution.py:108
  262.7 2.3 convert_reduce_fusion.1
  265.0 2.4 gather_fusion
  267.4 2.7 fusion.19
  270.1 4.4 %collective-permute-start = (bf16[1,128,3584]{2,1,0:T(8,128)(2,1)}, bf16[1,128,3584]{2,1,0:T(8,128)(2,1)}, u32[]{:S(2)}, u32[]{:S(2)}) collective-permute-start(bf16[1,128,3584]{2,1,0:T(8,128)(2,1)} %fusion.19), channel_id=1, source_target_pairs={{240,0},{0,16},{16,32},{32,48},{48,64},{64,80},{80,96},{96,112},{1... | collective-permute-start | bytes 2752520 | tf_op jit(solution)/shard_map/ppermute | solution.py:12
  274.5 36.2 %all-to-all-done.4 = bf16[8,40,3584]{2,1,0:T(8,128)(2,1)} async-done(((bf16[8,40,3584]{2,1,0:T(8,128)(2,1)}), bf16[8,40,3584]{2,1,0:T(8,128)(2,1)}, u32[]{:S(2)}, u32[]{:S(2)}) %all-to-all-start.4) | async-done | bytes 2293792 | tf_op jit(solution)/shard_map/all_to_all | solution.py:108
  310.7 2.3 convert_reduce_fusion
  312.9 2.4 gather_fusion.1
  317.4 6.9 %collective-permute-start.1 = (bf16[1,128,3584]{2,1,0:T(8,128)(2,1)S(1)}, bf16[1,128,3584]{2,1,0:T(8,128)(2,1)S(1)}, u32[]{:S(2)}, u32[]{:S(2)}) collective-permute-start(bf16[1,128,3584]{2,1,0:T(8,128)(2,1)S(1)} %fusion.15), channel_id=1, source_target_pairs={{16,0},{32,16},{48,32},{64,48},{80,64},{96,80},{112,96},{128,112},... | collective-permute-start | bytes 2752520 | tf_op jit(solution)/shard_map/ppermute | solution.py:12
  324.3 12.2 %collective-permute-done.1 = bf16[1,128,3584]{2,1,0:T(8,128)(2,1)S(1)} collective-permute-done((bf16[1,128,3584]{2,1,0:T(8,128)(2,1)S(1)}, bf16[1,128,3584]{2,1,0:T(8,128)(2,1)S(1)}, u32[]{:S(2)}, u32[]{:S(2)}) %collective-permute-start.1) | collective-permute-done | bytes 917536 | tf_op jit(solution)/shard_map/ppermute | solution.py:12
  (66 shorter events, 28.2 us)
Async XLA Ops:
  7.2 75.3 %copy-start = (bf16[1,128,3584]{2,1,0:T(8,128)(2,1)S(1)}, bf16[1,128,3584]{2,1,0:T(8,128)(2,1)}, u32[]{:S(2)}) copy-start(bf16[1,128,3584]{2,1,0:T(8,128)(2,1)} %param.13) | copy-start | bytes 2752516
  7.2 3.2 copy-start.5
  7.2 132.6 %all-gather.7.cloned.1.call-start = ((), (), s32[]{:S(2)}) async-start(), calls=%async_computation.7 | async-start | bytes 5505024 | tf_op jit(solution)/shard_map/all_gather | solution.py:76
  14.2 8.9 %copy-start.13 = (s32[1,128,1]{1,2,0:T(1,128)S(1)}, s32[1,128,1]{1,2,0:T(1,128)}, u32[]{:S(2)}) copy-start(s32[1,128,1]{1,2,0:T(1,128)} %param.15) | copy-start | bytes 1540
  14.2 9.3 %copy-start.3 = (bf16[1,128,3584]{2,1,0:T(8,128)(2,1)S(1)}, bf16[1,128,3584]{2,1,0:T(8,128)(2,1)}, u32[]{:S(2)}) copy-start(bf16[1,128,3584]{2,1,0:T(8,128)(2,1)} %param.14) | copy-start | bytes 2752516
  14.2 9.4 %copy-start.14 = (f32[1,128,1]{1,2,0:T(1,128)S(1)}, f32[1,128,1]{1,2,0:T(1,128)}, u32[]{:S(2)}) copy-start(f32[1,128,1]{1,2,0:T(1,128)} %param.16) | copy-start | bytes 1540
  14.2 61.6 %all-to-all-start = ((bf16[8,40,3584]{2,1,0:T(8,128)(2,1)}), bf16[8,40,3584]{2,1,0:T(8,128)(2,1)}, u32[]{:S(2)}, u32[]{:S(2)}) async-start(bf16[8,40,3584]{2,1,0:T(8,128)(2,1)} %bitcast.7), calls=%async_computation | async-start | bytes 4587520 | tf_op jit(solution)/shard_map/all_to_all | solution.py:95
  22.3 122.0 %all-gather.11.cloned.1.call-start = ((), (), s32[]{:S(2)}) async-start(), calls=%async_computation.9 | async-start | bytes 5505024 | tf_op jit(solution)/shard_map/all_gather | solution.py:78
  77.4 52.2 %all-to-all-start.2 = ((bf16[8,40,3584]{2,1,0:T(8,128)(2,1)}), bf16[8,40,3584]{2,1,0:T(8,128)(2,1)}, u32[]{:S(2)}, u32[]{:S(2)}) async-start(bf16[8,40,3584]{2,1,0:T(8,128)(2,1)} %bitcast.23), calls=%async_computation.2 | async-start | bytes 4587520 | tf_op jit(solution)/shard_map/all_to_all | solution.py:105
  81.7 105.7 %all-gather.9.cloned.1.call-start = ((), (), s32[]{:S(2)}) async-start(), calls=%async_computation.8 | async-start | bytes 5505024 | tf_op jit(solution)/shard_map/all_gather | solution.py:77
  131.2 64.1 %all-to-all-start.3 = ((bf16[8,40,3584]{2,1,0:T(8,128)(2,1)}), bf16[8,40,3584]{2,1,0:T(8,128)(2,1)S(1)}, u32[]{:S(2)}, u32[]{:S(2)}) async-start(bf16[8,40,3584]{2,1,0:T(8,128)(2,1)} %bitcast.27), calls=%async_computation.3 | async-start | bytes 4587520 | tf_op jit(solution)/shard_map/all_to_all | solution.py:104
  196.7 60.2 %all-to-all-start.1 = ((bf16[8,40,3584]{2,1,0:T(8,128)(2,1)}), bf16[8,40,3584]{2,1,0:T(8,128)(2,1)S(1)}, u32[]{:S(2)}, u32[]{:S(2)}) async-start(bf16[8,40,3584]{2,1,0:T(8,128)(2,1)} %bitcast.107), calls=%async_computation.1 | async-start | bytes 4587520 | tf_op jit(solution)/shard_map/all_to_all | solution.py:96
  203.6 132.8 %reduce-scatter.2.cloned.1.call-start = ((), (), s32[]{:S(2)}) async-start(), calls=%async_computation.6 | async-start | bytes 5505024 | tf_op jit(solution)/shard_map/reduce_scatter | solution.py:119
  203.6 4.2 %copy-start.4 = (bf16[1,3584,512]{2,1,0:T(8,128)(2,1)S(1)}, bf16[1,3584,512]{2,1,0:T(8,128)(2,1)}, u32[]{:S(2)}) copy-start(bf16[1,3584,512]{2,1,0:T(8,128)(2,1)} %all-gather.7.cloned.1.call-done) | copy-start | bytes 11010052
  203.6 4.5 %copy-start.10 = (bf16[8,40,3584]{2,1,0:T(8,128)(2,1)S(1)}, bf16[8,40,3584]{2,1,0:T(8,128)(2,1)}, u32[]{:S(2)}) copy-start(bf16[8,40,3584]{2,1,0:T(8,128)(2,1)} %copy-done.9) | copy-start | bytes 6881284
  208.2 2.0 copy-start.7
  215.6 3.6 %copy-start.8 = (bf16[1,3584,512]{2,1,0:T(8,128)(2,1)S(1)}, bf16[1,3584,512]{2,1,0:T(8,128)(2,1)}, u32[]{:S(2)}) copy-start(bf16[1,3584,512]{2,1,0:T(8,128)(2,1)} %all-gather.9.cloned.1.call-done) | copy-start | bytes 11010052
  215.7 3.6 %copy-start.12 = (f32[320,512]{1,0:T(8,128)S(1)}, f32[320,512]{1,0:T(8,128)}, u32[]{:S(2)}) copy-start(f32[320,512]{1,0:T(8,128)} %copy-done.11) | copy-start | bytes 1966084
  258.3 52.3 %all-to-all-start.4 = ((bf16[8,40,3584]{2,1,0:T(8,128)(2,1)}), bf16[8,40,3584]{2,1,0:T(8,128)(2,1)}, u32[]{:S(2)}, u32[]{:S(2)}) async-start(bf16[8,40,3584]{2,1,0:T(8,128)(2,1)} %bitcast.29), calls=%async_computation.4 | async-start | bytes 4587520 | tf_op jit(solution)/shard_map/all_to_all | solution.py:108
  265.0 2.4 copy-start.6
  265.0 2.4 copy-start.15
  270.1 54.2 %collective-permute-start = (bf16[1,128,3584]{2,1,0:T(8,128)(2,1)}, bf16[1,128,3584]{2,1,0:T(8,128)(2,1)}, u32[]{:S(2)}, u32[]{:S(2)}) collective-permute-start(bf16[1,128,3584]{2,1,0:T(8,128)(2,1)} %fusion.19), channel_id=1, source_target_pairs={{240,0},{0,16},{16,32},{32,48},{48,64},{64,80},{80,96},{96,112},{1... | collective-permute-start | bytes 2752520 | tf_op jit(solution)/shard_map/ppermute | solution.py:12
  315.4 24.2 %copy-start.1 = (bf16[1,128,3584]{2,1,0:T(8,128)(2,1)S(1)}, bf16[1,128,3584]{2,1,0:T(8,128)(2,1)}, u32[]{:S(2)}) copy-start(bf16[1,128,3584]{2,1,0:T(8,128)(2,1)} %param.13) | copy-start | bytes 2752516
  317.4 19.1 %collective-permute-start.1 = (bf16[1,128,3584]{2,1,0:T(8,128)(2,1)S(1)}, bf16[1,128,3584]{2,1,0:T(8,128)(2,1)S(1)}, u32[]{:S(2)}, u32[]{:S(2)}) collective-permute-start(bf16[1,128,3584]{2,1,0:T(8,128)(2,1)S(1)} %fusion.15), channel_id=1, source_target_pairs={{16,0},{32,16},{48,32},{64,48},{80,64},{96,80},{112,96},{128,112},... | collective-permute-start | bytes 2752520 | tf_op jit(solution)/shard_map/ppermute | solution.py:12
  (3 other events, 4.2 us)
Sparse Core Ops, SparseCore 0:
  9.8 60.0 all-gather.6
  71.7 56.9 all-gather.10
  130.5 56.8 all-gather.8
  215.8 55.4 reduce-scatter.1
where the time goes:
time: 349 us; the launch traced here: 346 us
  waiting for transfers between devices  223 us (64%)
  starting transfers between devices  43.7 us (13%)
  matrix products  29.7 us (9%)
  local copies, waits for them, and re-layouts  20.9 us (6%)
  other arithmetic  14.3 us (4%)
  between operations  14 us (4%)
    all_to_all x1, waiting for transfers between devices, per_device(): lax.all_to_all(f_buf, 'expert', split_axis=0, concat_axis=0, tiled=True)  50 us
    all_to_all x1, waiting for transfers between devices, per_device(): lax.all_to_all(z_buf, 'expert', split_axis=0, concat_axis=0, tiled=True)  45 us
    all_gather x1, waiting for transfers between devices, per_device(): lax.all_gather(up_w[0], 'dp', axis=0, tiled=True)  43.1 us
    all_to_all x1, waiting for transfers between devices, per_device(): lax.all_to_all(back, 'expert', split_axis=0, concat_axis=0, tiled=True)  36.2 us
    all_to_all x1, waiting for transfers between devices, per_device(): lax.all_to_all(expert_forward(received, w_gate, w_up, w_down), 'expert',...  34.9 us
    ppermute x2, waiting for transfers between devices, shifted(): return lax.ppermute(block, axis, route)  12.2 us
    ppermute x2, starting transfers between devices, shifted(): return lax.ppermute(block, axis, route)  11.3 us
    all_to_all x1, starting transfers between devices, per_device(): lax.all_to_all(x_buf, 'expert', split_axis=0, concat_axis=0, tiled=True)  8.61 us
  transfers between devices with their start and end apart: 11, of which 6 were waited for; matrix products, arithmetic and copies ran while one was open for 17% of the time, Pallas kernels for 0%

commit v1 on v0

v1 whole, which is shorter than its diff:
```python
import functools

import jax
import jax.numpy as jnp
from jax import lax
from jax.experimental import pallas as pl
from jax.experimental.pallas import tpu as pltpu
from jax.sharding import PartitionSpec as P

MESH = pl.DeviceIdType.MESH
BF16, F32 = jnp.bfloat16, jnp.float32
X, Z, FW = 0, 1, 2
BACK, OUT = 0, 1
STEP = 256
ROLES = 96

SEND_GROUPS = {X: ((0, 2), (2, 7)), Z: ((0, 7),), FW: ((0, 7),)}
BACK_GROUPS = {BACK: ((0, 7),), OUT: ((0, 4), (4, 7))}


def kernel(
    sections, holders, cap,
    fwd_in, fwd_ids, fwd_gates, bwd_in, bwd_grad, bwd_ids, bwd_gates, gate_w, up_w, down_w,
    fwd_next, bwd_next, gate_grad,
    raw, wts, packed, recv, sel, slots, gts, pout, pin, acc, hid, part, part_in, ret, fin, grad,
    local_sem, send_sem, recv_sem,
):
    rows = fwd_in.shape[1]
    half, units = gate_w.shape[1], gate_w.shape[2]
    unit = 2 * cap
    quad = 4 * unit
    s, z, q = lax.axis_index("pipe"), lax.axis_index("expert"), lax.axis_index("dp")
    odd = z % 2
    o = 2 * odd - 1

    def at_z(offset):
        return (s, (z + offset * o + holders) % holders, q)

    twin = (s, z, 1 - q)
    mate = at_z(-1)
    section_after, section_before = (s + 1) % sections, (s + sections - 1) % sections
    peers = [twin, mate, at_z(1), at_z(2), at_z(-2), at_z(3)]
    peers += [(t, z, d) for t in (section_after, section_before) for d in (q, 1 - q)]

    roles = []

    def send(src, dst, device):
        i = len(roles)
        copy = pltpu.make_async_remote_copy(
            src_ref=src, dst_ref=dst, send_sem=send_sem.at[i], recv_sem=recv_sem.at[i],
            device_id=device, device_id_type=MESH,
        )
        roles.append(copy)
        copy.start()
        return copy

    def block(j):
        return pl.ds(j * unit, unit)

    def cols(group):
        return pl.ds(group[0] * STEP, (group[1] - group[0]) * STEP)

    mine = pl.ds(pl.multiple_of(q * rows, rows), rows)
    own_half = pl.ds(pl.multiple_of(q * half, half), half)
    own_rows = pl.ds(pl.multiple_of(q * quad, quad), quad)
    other_rows = pl.ds(pl.multiple_of((1 - q) * quad, quad), quad)
    tokens = {X: bwd_in, Z: bwd_grad, FW: fwd_in}

    loads = {}
    for a in (X, Z, FW):
        loads[a] = pltpu.make_async_copy(
            tokens[a].at[0, :, own_half], raw.at[a, mine, :], local_sem.at[a]
        )
        loads[a].start()
    weight_loads = []
    for i, w in enumerate((gate_w, up_w, down_w)):
        weight_loads.append(pltpu.make_async_copy(w.at[0], wts.at[i], local_sem.at[3 + i]))
        weight_loads[-1].start()

    before = lax.broadcasted_iota(jnp.int32, (rows, rows), 0) < lax.broadcasted_iota(
        jnp.int32, (rows, rows), 1
    )
    pair = (z // 2).astype(F32)
    step_up = (2 - odd).astype(F32)
    step_down = (1 + odd).astype(F32)
    for i, (ids, gates) in enumerate(((bwd_ids, bwd_gates), (fwd_ids, fwd_gates))):
        down = jnp.broadcast_to(ids[0].astype(F32), (rows, rows))
        across = down.T
        same = jnp.where((down == across) & before, 1.0, 0.0)
        rank = jnp.sum(same, axis=0, keepdims=True)
        delta = across[0:1, :] - pair
        delta = jnp.where(delta < 0.0, delta + 4.0, delta)
        place = jnp.where(
            delta == 0.0, 0.0,
            jnp.where(delta == 2.0, 3.0, jnp.where(delta == 1.0, step_up, step_down)),
        )
        slot = place * unit + q.astype(F32) * cap + rank
        slots[q, pl.ds(8 * i, 8), :] = jnp.broadcast_to(slot, (8, rows))
        gts[q, i] = jnp.broadcast_to(gates[0], (rows, rows))

    barrier = pltpu.get_barrier_semaphore()
    for peer in peers:
        pl.semaphore_signal(barrier, inc=1, device_id=peer, device_id_type=MESH)
    pl.semaphore_wait(barrier, len(peers))

    meta = [send(slots.at[q], slots.at[q], twin), send(gts.at[q], gts.at[q], twin)]
    cross = {}
    for a in (X, Z, FW):
        for group in SEND_GROUPS[a]:
            width = (group[1] - group[0]) * STEP
            start = pl.multiple_of((1 - q) * half + group[0] * STEP, STEP)
            cross[a, group] = send(
                tokens[a].at[0, :, pl.ds(start, width)], raw.at[a, mine, cols(group)], twin
            )
    for copy in meta:
        copy.wait_recv()
    for i in range(2):
        for b in range(2):
            slot = slots[b, 8 * i : 8 * i + 1, :]
            index = lax.broadcasted_iota(jnp.int32, (quad, rows), 0).astype(F32)
            sel[i, :, b * rows : (b + 1) * rows] = jnp.where(index == slot, 1.0, 0.0).astype(BF16)

    direct, passed = {}, {}

    def pack(a):
        for group in SEND_GROUPS[a]:
            if group[0] == 0:
                loads[a].wait()
            cross[a, group].wait_recv()

            @pl.loop(group[0], group[1])
            def _(c):
                at = pl.ds(pl.multiple_of(c * STEP, STEP), STEP)
                block_in = raw[a, :, at]
                if a == Z:
                    gate = jnp.concatenate([gts[0, 0][:, 0:1], gts[1, 0][:, 0:1]], axis=0)
                    block_in = (gate * block_in.astype(F32)).astype(BF16)
                placed = jnp.dot(
                    sel[0 if a != FW else 1], block_in, preferred_element_type=F32
                ).astype(BF16)
                recv[a, 0:unit, at] = placed[0:unit]
                packed[a, :, at] = placed[unit:]

            w = cols(group)
            for j, offset in ((3, 3), (2, -2), (1, 1)):
                direct[a, group, j] = send(
                    packed.at[a, pl.ds((j - 1) * unit, unit), w], recv.at[a, block(j), w],
                    at_z(offset),
                )
            direct[a, group, 0] = send(recv.at[a, block(0), w], recv.at[a, block(7), w], mate)

    def pass_on(a):
        for group in SEND_GROUPS[a]:
            w = cols(group)
            for j in (1, 2, 3):
                direct[a, group, j].wait_recv()
                passed[a, group, j] = send(
                    recv.at[a, block(j), w], recv.at[a, block(7 - j), w], mate
                )

    def arrived(a):
        for group in SEND_GROUPS[a]:
            direct[a, group, 0].wait_recv()
            for j in (1, 2, 3):
                passed[a, group, j].wait_recv()

    def project(a, w, i):
        pout[i] = jnp.dot(recv[a, other_rows, :], wts[w], preferred_element_type=F32).astype(BF16)
        return send(pout.at[i], pin.at[i], twin)

    def project_own(a, w, i):
        acc[i] = jnp.dot(recv[a, own_rows, :], wts[w], preferred_element_type=F32)

    pack(X)
    pack(Z)
    pass_on(X)
    pack(FW)
    arrived(X)
    for load in weight_loads:
        load.wait()
    sums = {i: project(X, i, i) for i in (0, 1)}
    for i in (0, 1):
        project_own(X, i, i)
    pass_on(Z)
    arrived(Z)
    sums[2] = project(Z, 2, 2)
    project_own(Z, 2, 2)
    pass_on(FW)
    for i in range(3):
        sums[i].wait_recv()

    tile = 32

    @pl.loop(0, quad // tile)
    def _(r):
        at = pl.ds(pl.multiple_of(r * tile, tile), tile)
        to = pl.ds(pl.multiple_of(q * quad + r * tile, tile), tile)
        gate = acc[0, at, :] + pin[0, at, :].astype(F32)
        up = acc[1, at, :] + pin[1, at, :].astype(F32)
        dh = acc[2, at, :] + pin[2, at, :].astype(F32)
        sigma = jax.nn.sigmoid(gate)
        hid[0, to, :] = (dh * up * sigma * (1.0 + gate * (1.0 - sigma))).astype(BF16)
        hid[1, to, :] = (dh * (gate * sigma)).astype(BF16)

    shared = {i: send(hid.at[i, own_rows, :], hid.at[i, own_rows, :], twin) for i in (0, 1)}

    def expand(r, group, terms, lo):
        @pl.loop(group[0], group[1])
        def _(c):
            at = pl.ds(pl.multiple_of(c * STEP, STEP), STEP)
            total = None
            for i, w in terms:
                term = lax.dot_general(
                    hid[i, lo : lo + quad, :], wts[w, at, :], (((1,), (1,)), ((), ())),
                    preferred_element_type=F32,
                )
                total = term if total is None else total + term
            part[r, lo : lo + quad, at] = total.astype(BF16)

    halves, returned = {}, {}

    def give(r, terms):
        for group in BACK_GROUPS[r]:
            expand(r, group, terms, quad)
            w = cols(group)
            for j in (4, 5, 6, 7):
                halves[r, group, j] = send(
                    part.at[r, block(j), w], part_in.at[r, block(7 - j), w], mate
                )
        for group in BACK_GROUPS[r]:
            expand(r, group, terms, 0)

    def merge(r):
        for group in BACK_GROUPS[r]:
            w = cols(group)
            for j, offset in ((3, 3), (2, 2), (1, 1), (0, 0)):
                halves[r, group, 7 - j].wait_recv()

                @pl.loop(group[0], group[1])
                def _(c):
                    at = pl.ds(pl.multiple_of(c * STEP, STEP), STEP)
                    total = (
                        part[r, block(j), at].astype(F32) + part_in[r, block(j), at].astype(F32)
                    ).astype(BF16)
                    if j == 0:
                        ret[r, block(0), at] = total
                    else:
                        part[r, block(j), at] = total

                if j:
                    returned[r, group, j] = send(
                        part.at[r, block(j), w], ret.at[r, block(j), w], at_z(offset)
                    )

    last = []

    def finish(r):
        a, i, section, target = (
            (Z, 0, section_before, bwd_next) if r == BACK else (FW, 1, section_after, fwd_next)
        )
        for group in BACK_GROUPS[r]:
            for j in (1, 2, 3):
                returned[r, group, j].wait_recv()

            @pl.loop(group[0], group[1])
            def _(c):
                at = pl.ds(pl.multiple_of(c * STEP, STEP), STEP)
                picked = lax.dot_general(
                    sel[i], ret[r, :, at], (((0,), (0,)), ((), ())), preferred_element_type=F32
                )
                if r == OUT:
                    gate = jnp.concatenate([gts[0, 1][:, 0:1], gts[1, 1][:, 0:1]], axis=0)
                    picked = gate * picked
                fin[r, :, at] = (raw[a, :, at].astype(F32) + picked).astype(BF16)

            width = (group[1] - group[0]) * STEP
            start = pl.multiple_of(q * half + group[0] * STEP, STEP)
            for device in (1 - q, q):
                from_rows = pl.ds(pl.multiple_of(device * rows, rows), rows)
                last.append(
                    send(
                        fin.at[r, from_rows, cols(group)],
                        target.at[0, :, pl.ds(start, width)],
                        (section, z, device),
                    )
                )

    for i in (0, 1):
        shared[i].wait_recv()
    give(BACK, ((0, 0), (1, 1)))

    arrived(FW)
    for i in (0, 1):
        sums[3 + i] = project(FW, i, 3 + i)
    merge(BACK)
    for i in (0, 1):
        project_own(FW, i, i)
    for i in (3, 4):
        sums[i].wait_recv()

    @pl.loop(0, quad // tile)
    def _(r):
        at = pl.ds(pl.multiple_of(r * tile, tile), tile)
        to = pl.ds(pl.multiple_of(q * quad + r * tile, tile), tile)
        gate = acc[0, at, :] + pin[3, at, :].astype(F32)
        up = acc[1, at, :] + pin[4, at, :].astype(F32)
        hid[2, to, :] = (gate * jax.nn.sigmoid(gate) * up).astype(BF16)

    shared[2] = send(hid.at[2, own_rows, :], hid.at[2, own_rows, :], twin)

    @pl.loop(0, half // STEP)
    def _(c):
        at = pl.ds(pl.multiple_of(c * STEP, STEP), STEP)
        grad[at, :] = lax.dot_general(
            recv[X, :, at], hid[0], (((0,), (0,)), ((), ())), preferred_element_type=F32
        ).astype(BF16)

    store = pltpu.make_async_copy(grad, gate_grad.at[0], local_sem.at[6])
    store.start()
    shared[2].wait_recv()
    give(OUT, ((2, 2),))
    merge(OUT)
    finish(BACK)
    finish(OUT)
    for copy in last:
        copy.wait_recv()
    for copy in roles:
        copy.wait_send()
    store.wait()


def per_device(
    fwd_in, fwd_ids, fwd_gates, bwd_in, bwd_grad, bwd_ids, bwd_gates, gate_w, up_w, down_w
):
    sections, holders = lax.axis_size("pipe"), lax.axis_size("expert")
    rows, width = fwd_in.shape[1], fwd_in.shape[2]
    half, units = gate_w.shape[1], gate_w.shape[2]
    experts = holders // 2
    cap = rows * 5 // (4 * experts)
    quad = 8 * cap
    hbm = pl.BlockSpec(memory_space=pl.ANY)
    vmem = pl.BlockSpec(memory_space=pltpu.VMEM)
    return pl.pallas_call(
        functools.partial(kernel, sections, holders, cap),
        out_shape=(
            jax.ShapeDtypeStruct(fwd_in.shape, BF16),
            jax.ShapeDtypeStruct(bwd_in.shape, BF16),
            jax.ShapeDtypeStruct(gate_w.shape, BF16),
        ),
        in_specs=[hbm, vmem, vmem, hbm, hbm, vmem, vmem, hbm, hbm, hbm],
        out_specs=(hbm, hbm, hbm),
        scratch_shapes=[
            pltpu.VMEM((3, 2 * rows, half), BF16),
            pltpu.VMEM((3, half, units), BF16),
            pltpu.VMEM((3, 6 * cap, half), BF16),
            pltpu.VMEM((3, 2 * quad, half), BF16),
            pltpu.VMEM((2, quad, 2 * rows), BF16),
            pltpu.VMEM((2, 16, rows), F32),
            pltpu.VMEM((2, 2, rows, rows), F32),
            pltpu.VMEM((5, quad, units), BF16),
            pltpu.VMEM((5, quad, units), BF16),
            pltpu.VMEM((3, quad, units), F32),
            pltpu.VMEM((3, 2 * quad, units), BF16),
            pltpu.VMEM((2, 2 * quad, half), BF16),
            pltpu.VMEM((2, quad, half), BF16),
            pltpu.VMEM((2, quad, half), BF16),
            pltpu.VMEM((2, 2 * rows, half), BF16),
            pltpu.VMEM((half, units), BF16),
            pltpu.SemaphoreType.DMA((7,)),
            pltpu.SemaphoreType.DMA((ROLES,)),
            pltpu.SemaphoreType.DMA((ROLES,)),
        ],
        compiler_params=pltpu.CompilerParams(
            collective_id=0, has_side_effects=True, vmem_limit_bytes=60 << 20
        ),
        name="routed_layer",
    )(fwd_in, fwd_ids, fwd_gates, bwd_in, bwd_grad, bwd_ids, bwd_gates, gate_w, up_w, down_w)


def solution(mesh):
    tokens = P("pipe", ("expert", "dp"), None)
    weights = P("pipe", "dp", "expert")
    return jax.shard_map(
        per_device,
        mesh=mesh,
        in_specs=(tokens,) * 7 + (weights,) * 3,
        out_specs=(tokens, tokens, weights),
        check_vma=False,
    )
```

time: 349 us -> 262 us (0.75)
  the two profiles are of different devices: /device:TPU:33 before, /device:TPU:237 now
where the time goes in v1:
time: 262 us
  Pallas kernels  252 us (96%)
  local copies, waits for them, and re-layouts  10 us (4%)
    pallas_call x1, Pallas kernels, per_device(): pl.pallas_call(functools.partial(kernel, sections, holders, cap), out_sha...  252 us
    unnamed x11, local copies, waits for them, and re-layouts  10 us

profile of v1, /device:TPU:237, one launch (start us, length us, event | category | flops | bytes accessed | tf_op | source)
XLA Modules:
  0.0 262.2 jit_solution(12168394851868322839)
XLA Ops:
  0.6 1.4 copy.13.fwd_ids
  2.0 1.4 copy.14.fwd_gates
  3.4 1.4 copy.15.bwd_ids
  4.8 1.4 copy.16.bwd_gates
  6.2 251.5 %routed_layer.1 = (bf16[1,128,3584]{2,1,0:T(8,128)(2,1)}, bf16[1,128,3584]{2,1,0:T(8,128)(2,1)}, bf16[1,1792,512]{2,1,0:T(8,128)(2,1)}) custom-call(bf16[1,128,3584]{2,1,0:T(8,128)(2,1)} %fwd_in.1, s32[1,128,1]{2,1,0:T(8,128)} %copy.13.fwd_ids, f32[1,128,1]{2,1,0:T(8,128)} %copy.14.fwd_gates, bf16[1,128,3584]{2,1,0:T(8,128)(2,1)} %bwd_in.1, ...), custom_call_target="tpu_custom_call" | custom-call | tf_op jit(solution)/shard_map/routed_layer/pallas_call | solution.py:343
  257.7 0.0 copy-start.1
  257.7 0.0 copy-start
  257.7 2.3 copy.20
  260.0 0.0 copy-done.1
  260.0 0.9 copy.21
  261.0 0.0 copy-done
  261.0 1.2 copy.22
Async XLA Ops:
  257.7 2.3 copy-start.1
  257.7 3.2 %copy-start = (bf16[1,1792,512]{2,1,0:T(8,128)(2,1)S(1)}, bf16[1,1792,512]{2,1,0:T(8,128)(2,1)}, u32[]{:S(2)}) copy-start(bf16[1,1792,512]{2,1,0:T(8,128)(2,1)} %get-tuple-element.8) | copy-start | bytes 5505028

commit v2 on v1

v2 whole, which is shorter than its diff:
```python
import functools

import jax
import jax.numpy as jnp
from jax import lax
from jax.experimental import pallas as pl
from jax.experimental.pallas import tpu as pltpu
from jax.sharding import PartitionSpec as P

MESH = pl.DeviceIdType.MESH
BF16, F32 = jnp.bfloat16, jnp.float32
X, Z, FW = 0, 1, 2
BACK, OUT = 0, 1
STEP = 256
ROLES = 128
PLACE = {0: 0, 3: 1, 4: 2, 7: 3, 1: 4, 2: 5, 5: 6, 6: 7}

ALL, OWN, REST = 0, 1, 2
SEND_GROUPS = {
    FW: ((0, 7, OWN), (0, 3, REST), (3, 7, REST)),
    X: ((0, 3, ALL), (3, 7, ALL)),
    Z: ((0, 7, ALL),),
}
BACK_GROUPS = {OUT: ((0, 4), (4, 7)), BACK: ((0, 2), (2, 4), (4, 6), (6, 7))}


def kernel(
    sections, holders, cap,
    fwd_in, fwd_ids, fwd_gates, bwd_in, bwd_grad, bwd_ids, bwd_gates, gate_w, up_w, down_w,
    fwd_next, bwd_next, gate_grad,
    raw, wts, packed, recv, sel, slots, gts, pout, pin, acc, hid, part, part_in, ret, fin, grad,
    local_sem, send_sem, recv_sem,
):
    rows = fwd_in.shape[1]
    half, units = gate_w.shape[1], gate_w.shape[2]
    unit = 2 * cap
    quad = 4 * unit
    head = cap - cap % 16
    s, z, q = lax.axis_index("pipe"), lax.axis_index("expert"), lax.axis_index("dp")
    odd = z % 2
    o = 2 * odd - 1

    def at_z(offset):
        return (s, (z + offset * o + holders) % holders, q)

    twin = (s, z, 1 - q)
    mate = at_z(-1)
    section_after, section_before = (s + 1) % sections, (s + sections - 1) % sections
    peers = [twin, mate, at_z(1), at_z(2), at_z(-2), at_z(3)]
    peers += [(t, z, d) for t in (section_after, section_before) for d in (q, 1 - q)]

    roles = []

    def describe(src, dst, device):
        i = len(roles)
        copy = pltpu.make_async_remote_copy(
            src_ref=src, dst_ref=dst, send_sem=send_sem.at[i], recv_sem=recv_sem.at[i],
            device_id=device, device_id_type=MESH,
        )
        roles.append(copy)
        return copy

    def send(src, dst, device):
        copy = describe(src, dst, device)
        copy.start()
        return copy

    def block(j):
        return pl.ds(PLACE[j] * unit, unit)

    def slot_of(j):
        return pl.ds(j * unit, unit)

    def mate_rows(d):
        return pl.ds(pl.multiple_of(d * quad + 2 * unit, 2 * unit), 2 * unit)

    def kept_rows(d):
        return pl.ds(pl.multiple_of(d * quad, 2 * unit), 2 * unit)

    def cols(group):
        return pl.ds(group[0] * STEP, (group[1] - group[0]) * STEP)

    mine = pl.ds(pl.multiple_of(q * rows, rows), rows)
    own_half = pl.ds(pl.multiple_of(q * half, half), half)
    own_rows = pl.ds(pl.multiple_of(q * quad, quad), quad)
    other_rows = pl.ds(pl.multiple_of((1 - q) * quad, quad), quad)
    tokens = {X: bwd_in, Z: bwd_grad, FW: fwd_in}

    loads = {}
    for a in (FW, X, Z):
        loads[a] = pltpu.make_async_copy(
            tokens[a].at[0, :, own_half], raw.at[a, mine, :], local_sem.at[a]
        )
        loads[a].start()
    weight_loads = []
    for i, w in enumerate((gate_w, up_w, down_w)):
        weight_loads.append(pltpu.make_async_copy(w.at[0], wts.at[i], local_sem.at[3 + i]))
        weight_loads[-1].start()

    before = lax.broadcasted_iota(jnp.int32, (rows, rows), 0) < lax.broadcasted_iota(
        jnp.int32, (rows, rows), 1
    )
    pair = (z // 2).astype(F32)
    step_up = (2 - odd).astype(F32)
    step_down = (1 + odd).astype(F32)
    for i, (ids, gates) in enumerate(((bwd_ids, bwd_gates), (fwd_ids, fwd_gates))):
        across = jnp.broadcast_to(ids[0].astype(F32), (rows, rows))
        down = across.T
        same = jnp.where((down == across) & before, 1.0, 0.0)
        rank = jnp.sum(same, axis=0, keepdims=True)
        delta = across[0:1, :] - pair
        delta = jnp.where(delta < 0.0, delta + 4.0, delta)
        place = jnp.where(
            delta == 0.0, 0.0,
            jnp.where(delta == 2.0, 3.0, jnp.where(delta == 1.0, step_up, step_down)),
        )
        side = q.astype(F32)
        within = jnp.where(
            rank < head, side * (unit - head) + rank, head + side * (cap - head) + rank - head
        )
        slot = place * unit + within
        slots[q, pl.ds(8 * i, 8), :] = jnp.broadcast_to(slot, (8, rows))
        slots[q, pl.ds(8 * i + 16, 8), :] = jnp.broadcast_to(gates[0], (8, rows))

    index = lax.broadcasted_iota(jnp.int32, (quad, rows), 0).astype(F32)

    def select(i, b):
        slot = slots[b, 8 * i : 8 * i + 1, :]
        at = pl.ds(pl.multiple_of(b * rows, rows), rows)
        sel[i, :, at] = jnp.where(index == slot, 1.0, 0.0).astype(BF16)

    def piece(kind):
        if kind == ALL:
            return 0, unit
        if kind == OWN:
            return pl.multiple_of(q * (unit - head), 16), head
        return pl.multiple_of((1 - q) * head, 16), unit - head

    def place_rows(a, lo, hi, kind, tokens_at):
        start, size = piece(kind)
        i = 0 if a != FW else 1
        if kind == ALL:
            chosen = sel[i]
        else:
            chosen = jnp.concatenate(
                [sel[i, pl.ds(j * unit + start, size), tokens_at] for j in range(4)], axis=0
            )

        @pl.loop(lo, hi)
        def _(c):
            at = pl.ds(pl.multiple_of(c * STEP, STEP), STEP)
            block_in = raw[a, tokens_at, at]
            if a == Z:
                gate = jnp.concatenate([gts[0, 0][:, 0:1], gts[1, 0][:, 0:1]], axis=0)
                block_in = (gate * block_in.astype(F32)).astype(BF16)
            placed = jnp.dot(chosen, block_in, preferred_element_type=F32).astype(BF16)
            recv[a, pl.ds(start, size), at] = placed[0:size]
            for j in (1, 2, 3):
                packed[a, pl.ds((j - 1) * unit + start, size), at] = placed[j * size : (j + 1) * size]

    loads[FW].wait()
    select(1, q)
    place_rows(FW, 0, half // STEP, OWN, mine)

    barrier = pltpu.get_barrier_semaphore()
    for peer in peers:
        pl.semaphore_signal(barrier, inc=1, device_id=peer, device_id_type=MESH)
    pl.semaphore_wait(barrier, len(peers))

    meta = send(slots.at[q], slots.at[q], twin)
    cross = {}
    for a in (FW, X, Z):
        for group in SEND_GROUPS[a]:
            if group[2] == OWN:
                continue
            width = (group[1] - group[0]) * STEP
            start = pl.multiple_of((1 - q) * half + group[0] * STEP, STEP)
            cross[a, group] = send(
                tokens[a].at[0, :, pl.ds(start, width)], raw.at[a, mine, cols(group)], twin
            )
    direct, passed = {}, {}

    def part_of(ref, a, row, group):
        start, size = piece(group[2])
        return ref.at[a, pl.ds(row + start, size), cols(group)]

    def dispatch(a, n):
        group = SEND_GROUPS[a][n]
        for j, offset in ((2, -2), (0, -1), (3, 3), (1, 1)):
            source = (
                part_of(packed, a, (j - 1) * unit, group) if j else part_of(recv, a, 0, group)
            )
            row = PLACE[j if j else 7] * unit
            direct[a, group, j] = send(source, part_of(recv, a, row, group), at_z(offset))

    def pack(a, n):
        group = SEND_GROUPS[a][n]
        if group[0] == 0 and a != FW:
            loads[a].wait()
        cross[a, group].wait_recv()
        place_rows(a, *group, pl.ds(0, 2 * rows))
        dispatch(a, n)

    def pass_on(a, n):
        group = SEND_GROUPS[a][n]
        for j in (1, 2, 3):
            direct[a, group, j].wait_recv()
            passed[a, group, j] = send(
                part_of(recv, a, PLACE[j] * unit, group),
                part_of(recv, a, PLACE[7 - j] * unit, group),
                mate,
            )

    def arrived(a):
        for group in SEND_GROUPS[a]:
            direct[a, group, 0].wait_recv()
            for j in (1, 2, 3):
                passed[a, group, j].wait_recv()

    dispatch(FW, 0)
    meta.wait_recv()
    select(1, 1 - q)
    for b in range(2):
        for i in range(2):
            gate = slots[b, 8 * i + 16 : 8 * i + 17, :]
            gts[b, i] = jnp.broadcast_to(gate, (rows, rows)).T
        select(0, b)

    def project(a, w, i):
        pout[i] = jnp.dot(recv[a, other_rows, :], wts[w], preferred_element_type=F32).astype(BF16)
        return send(pout.at[i], pin.at[i], twin)

    def project_own(a, w, i):
        acc[i] = jnp.dot(recv[a, own_rows, :], wts[w], preferred_element_type=F32)

    pass_on(FW, 0)
    pack(FW, 1)
    pack(FW, 2)
    pass_on(FW, 1)
    pack(X, 0)
    pack(X, 1)
    pass_on(FW, 2)
    pack(Z, 0)
    pass_on(X, 0)
    arrived(FW)
    for load in weight_loads:
        load.wait()
    sums = {3 + i: project(FW, i, 3 + i) for i in (0, 1)}
    for i in (0, 1):
        project_own(FW, i, i)
    pass_on(X, 1)
    for i in (3, 4):
        sums[i].wait_recv()

    tile = 32

    @pl.loop(0, quad // tile)
    def _(r):
        at = pl.ds(pl.multiple_of(r * tile, tile), tile)
        to = pl.ds(pl.multiple_of(q * quad + r * tile, tile), tile)
        gate = acc[0, at, :] + pin[3, at, :].astype(F32)
        up = acc[1, at, :] + pin[4, at, :].astype(F32)
        hid[2, to, :] = (gate * jax.nn.sigmoid(gate) * up).astype(BF16)

    shared = {2: send(hid.at[2, own_rows, :], hid.at[2, own_rows, :], twin)}

    def expand(r, group, terms, rows_of):
        @pl.loop(group[0], group[1])
        def _(c):
            at = pl.ds(pl.multiple_of(c * STEP, STEP), STEP)
            total = None
            for i, w in terms:
                term = lax.dot_general(
                    hid[i, rows_of, :], wts[w, at, :], (((1,), (1,)), ((), ())),
                    preferred_element_type=F32,
                )
                total = term if total is None else total + term
            part[r, rows_of, at] = total.astype(BF16)

    halves, returned = {}, {}

    def give(r, n, d, step):
        w = cols(BACK_GROUPS[r][n])
        for i, row in enumerate((3 - d, d)):
            source = pl.ds(pl.multiple_of(d * quad + (2 + i) * unit, unit), unit)
            target = pl.ds(pl.multiple_of(row * unit, unit), unit)
            halves[r, n, step, i] = send(part.at[r, source, w], part_in.at[r, target, w], mate)

    def merge(r, n, d, step):
        group = BACK_GROUPS[r][n]
        w = cols(group)
        for i, row in enumerate((3 - d, d)):
            halves[r, n, step, i].wait_recv()
            kept = pl.ds(pl.multiple_of(d * quad + (1 - i) * unit, unit), unit)
            slot = pl.ds(pl.multiple_of(row * unit, unit), unit)

            @pl.loop(group[0], group[1])
            def _(c):
                at = pl.ds(pl.multiple_of(c * STEP, STEP), STEP)
                part[r, kept, at] = (
                    part[r, kept, at].astype(F32) + part_in[r, slot, at].astype(F32)
                ).astype(BF16)

            if i == 0:
                returned[r, n, step] = send(
                    part.at[r, kept, w], ret.at[r, slot, w], at_z(3 - d)
                )
                continue
            if (r, n, 2) not in returned:
                returned[r, n, 2] = describe(
                    part.at[r, block(1), w], ret.at[r, slot_of(1), w], at_z(1)
                )

            @pl.when(d == 1)
            def _():
                returned[r, n, 2].start()

            @pl.when(d == 0)
            def _():
                ret[r, slot_of(0), w] = part[r, block(0), w]

    last = []

    def finish(r, n):
        a, i, section, target = (
            (Z, 0, section_before, bwd_next) if r == BACK else (FW, 1, section_after, fwd_next)
        )
        group = BACK_GROUPS[r][n]
        for j in (0, 1, 2):
            returned[r, n, j].wait_recv()
        for c in range(group[0], group[1], 2):
            at = cols((c, min(c + 2, group[1])))
            picked = lax.dot_general(
                sel[i], ret[r, :, at], (((0,), (0,)), ((), ())), preferred_element_type=F32
            )
            if r == OUT:
                gate = jnp.concatenate([gts[0, 1][:, 0:1], gts[1, 1][:, 0:1]], axis=0)
                picked = gate * picked
            fin[r, :, at] = (raw[a, :, at].astype(F32) + picked).astype(BF16)

        width = (group[1] - group[0]) * STEP
        start = pl.multiple_of(q * half + group[0] * STEP, STEP)
        for device in (1 - q, q):
            from_rows = pl.ds(pl.multiple_of(device * rows, rows), rows)
            last.append(
                send(
                    fin.at[r, from_rows, cols(group)],
                    target.at[0, :, pl.ds(start, width)],
                    (section, z, device),
                )
            )

    arrived(X)
    for i in (0, 1):
        sums[i] = project(X, i, i)
    for i in (0, 1):
        project_own(X, i, i)
    shared[2].wait_recv()
    for n, group in enumerate(BACK_GROUPS[OUT]):
        for d in (q, 1 - q):
            expand(OUT, group, ((2, 2),), mate_rows(d))
        if n == 0:
            for step, d in enumerate((q, 1 - q)):
                give(OUT, 0, d, step)
    pass_on(Z, 0)
    for n in range(1, len(BACK_GROUPS[OUT])):
        for step, d in enumerate((q, 1 - q)):
            give(OUT, n, d, step)
    for group in BACK_GROUPS[OUT]:
        for d in (q, 1 - q):
            expand(OUT, group, ((2, 2),), kept_rows(d))
    for step, d in enumerate((q, 1 - q)):
        merge(OUT, 0, d, step)
    arrived(Z)
    sums[2] = project(Z, 2, 2)
    project_own(Z, 2, 2)
    for i in range(3):
        sums[i].wait_recv()

    @pl.loop(0, quad // tile)
    def _(r):
        at = pl.ds(pl.multiple_of(r * tile, tile), tile)
        to = pl.ds(pl.multiple_of(q * quad + r * tile, tile), tile)
        gate = acc[0, at, :] + pin[0, at, :].astype(F32)
        up = acc[1, at, :] + pin[1, at, :].astype(F32)
        dh = acc[2, at, :] + pin[2, at, :].astype(F32)
        sigma = jax.nn.sigmoid(gate)
        hid[0, to, :] = (dh * up * sigma * (1.0 + gate * (1.0 - sigma))).astype(BF16)
        hid[1, to, :] = (dh * (gate * sigma)).astype(BF16)

    def share(rows_of):
        return [send(hid.at[i, rows_of, :], hid.at[i, rows_of, :], twin) for i in (0, 1)]

    back_terms = ((0, 0), (1, 1))
    back_groups = BACK_GROUPS[BACK]
    first = share(mate_rows(q))
    for n, group in enumerate(back_groups):
        expand(BACK, group, back_terms, mate_rows(q))
        give(BACK, n, q, 0)
    second = share(kept_rows(q))
    for group in back_groups:
        expand(BACK, group, back_terms, kept_rows(q))
    for step, d in enumerate((q, 1 - q)):
        merge(OUT, 1, d, step)
    finish(OUT, 0)
    for copy in first:
        copy.wait_recv()
    for n, group in enumerate(back_groups):
        expand(BACK, group, back_terms, mate_rows(1 - q))
        give(BACK, n, 1 - q, 1)
    for n in range(len(back_groups)):
        merge(BACK, n, q, 0)
    for copy in second:
        copy.wait_recv()
    for group in back_groups:
        expand(BACK, group, back_terms, kept_rows(1 - q))
    @pl.loop(0, half // STEP)
    def _(c):
        at = pl.ds(pl.multiple_of(c * STEP, STEP), STEP)
        grad[at, :] = lax.dot_general(
            recv[X, :, at], hid[0], (((0,), (0,)), ((), ())), preferred_element_type=F32
        ).astype(BF16)

    store = pltpu.make_async_copy(grad, gate_grad.at[0], local_sem.at[6])
    store.start()
    finish(OUT, 1)
    merge(BACK, 0, 1 - q, 1)
    merge(BACK, 1, 1 - q, 1)
    finish(BACK, 0)
    merge(BACK, 2, 1 - q, 1)
    finish(BACK, 1)
    merge(BACK, 3, 1 - q, 1)
    finish(BACK, 2)
    finish(BACK, 3)
    for copy in last:
        copy.wait_recv()
    for copy in roles:
        copy.wait_send()
    store.wait()


def across(column):
    return jnp.transpose(column, (0, 2, 1))


def per_device(
    fwd_in, fwd_ids, fwd_gates, bwd_in, bwd_grad, bwd_ids, bwd_gates, gate_w, up_w, down_w
):
    sections, holders = lax.axis_size("pipe"), lax.axis_size("expert")
    rows, width = fwd_in.shape[1], fwd_in.shape[2]
    half, units = gate_w.shape[1], gate_w.shape[2]
    experts = holders // 2
    cap = rows * 5 // (4 * experts)
    quad = 8 * cap
    hbm = pl.BlockSpec(memory_space=pl.ANY)
    vmem = pl.BlockSpec(memory_space=pltpu.VMEM)
    return pl.pallas_call(
        functools.partial(kernel, sections, holders, cap),
        out_shape=(
            jax.ShapeDtypeStruct(fwd_in.shape, BF16),
            jax.ShapeDtypeStruct(bwd_in.shape, BF16),
            jax.ShapeDtypeStruct(gate_w.shape, BF16),
        ),
        in_specs=[hbm, vmem, vmem, hbm, hbm, vmem, vmem, hbm, hbm, hbm],
        out_specs=(hbm, hbm, hbm),
        scratch_shapes=[
            pltpu.VMEM((3, 2 * rows, half), BF16),
            pltpu.VMEM((3, half, units), BF16),
            pltpu.VMEM((3, 6 * cap, half), BF16),
            pltpu.VMEM((3, 2 * quad, half), BF16),
            pltpu.VMEM((2, quad, 2 * rows), BF16),
            pltpu.VMEM((2, 32, rows), F32),
            pltpu.VMEM((2, 2, rows, rows), F32),
            pltpu.VMEM((5, quad, units), BF16),
            pltpu.VMEM((5, quad, units), BF16),
            pltpu.VMEM((3, quad, units), F32),
            pltpu.VMEM((3, 2 * quad, units), BF16),
            pltpu.VMEM((2, 2 * quad, half), BF16),
            pltpu.VMEM((2, quad, half), BF16),
            pltpu.VMEM((2, quad, half), BF16),
            pltpu.VMEM((2, 2 * rows, half), BF16),
            pltpu.VMEM((half, units), BF16),
            pltpu.SemaphoreType.DMA((7,)),
            pltpu.SemaphoreType.DMA((ROLES,)),
            pltpu.SemaphoreType.DMA((ROLES,)),
        ],
        compiler_params=pltpu.CompilerParams(
            collective_id=0, has_side_effects=True, vmem_limit_bytes=60 << 20
        ),
        name="routed_layer",
    )(
        fwd_in, across(fwd_ids), across(fwd_gates), bwd_in, bwd_grad, across(bwd_ids),
        across(bwd_gates), gate_w, up_w, down_w,
    )


def solution(mesh):
    tokens = P("pipe", ("expert", "dp"), None)
    weights = P("pipe", "dp", "expert")
    return jax.shard_map(
        per_device,
        mesh=mesh,
        in_specs=(tokens,) * 7 + (weights,) * 3,
        out_specs=(tokens, tokens, weights),
        check_vma=False,
    )
```

time: 262 us -> 225 us (0.86)
  the two profiles are of different devices: /device:TPU:237 before, /device:TPU:33 now
where the time goes in v2:
time: 225 us
  Pallas kernels  220 us (98%)
  local copies, waits for them, and re-layouts  4.47 us (2%)
    pallas_call x1, Pallas kernels, per_device(): pl.pallas_call(functools.partial(kernel, sections, holders, cap), out_sha...  220 us

profile of v2, /device:TPU:33, one launch (start us, length us, event | category | flops | bytes accessed | tf_op | source)
XLA Modules:
  0.0 225.4 jit_solution(11029469495852555874)
XLA Ops:
  0.6 220.2 %routed_layer.1 = (bf16[1,128,3584]{2,1,0:T(8,128)(2,1)}, bf16[1,128,3584]{2,1,0:T(8,128)(2,1)}, bf16[1,1792,512]{2,1,0:T(8,128)(2,1)}) custom-call(bf16[1,128,3584]{2,1,0:T(8,128)(2,1)} %fwd_in.1, s32[1,1,128]{2,1,0:T(1,128)} %bitcast.4, f32[1,1,128]{2,1,0:T(1,128)} %bitcast.5, bf16[1,128,3584]{2,1,0:T(8,128)(2,1)} %bwd_in.1, ...), custom_call_target="tpu_custom_call" | custom-call | tf_op jit(solution)/shard_map/routed_layer/pallas_call | solution.py:457
  220.9 0.0 copy-start.1
  220.9 0.0 copy-start
  220.9 2.3 %copy.16 = bf16[1,128,3584]{2,1,0:T(8,128)(2,1)} copy(bf16[1,128,3584]{2,1,0:T(8,128)(2,1)} %get-tuple-element.6) | data formatting | bytes 1835008
  223.2 0.0 copy-done.1
  223.2 0.9 copy.17
  224.1 0.0 copy-done
  224.1 1.2 copy.18
Async XLA Ops:
  220.9 2.3 %copy-start.1 = (bf16[1,128,3584]{2,1,0:T(8,128)(2,1)S(1)}, bf16[1,128,3584]{2,1,0:T(8,128)(2,1)}, u32[]{:S(2)}) copy-start(bf16[1,128,3584]{2,1,0:T(8,128)(2,1)} %get-tuple-element.7) | copy-start | bytes 2752516
  220.9 3.2 %copy-start = (bf16[1,1792,512]{2,1,0:T(8,128)(2,1)S(1)}, bf16[1,1792,512]{2,1,0:T(8,128)(2,1)}, u32[]{:S(2)}) copy-start(bf16[1,1792,512]{2,1,0:T(8,128)(2,1)} %get-tuple-element.8) | copy-start | bytes 5505028

commit v3 on v2

--- a/solution.py
+++ b/solution.py
@@ -439,6 +439,22 @@
     store.wait()
 
 
+def hand_over(*refs):
+    copies = []
+    for i in range(3):
+        rows = refs[i].shape[1] // 4
+        for j in range(4):
+            part = pl.ds(j * rows, rows)
+            copies.append(
+                pltpu.make_async_copy(
+                    refs[i].at[0, part], refs[3 + i].at[0, part], refs[6].at[4 * i + j]
+                )
+            )
+            copies[-1].start()
+    for copy in copies:
+        copy.wait()
+
+
 def across(column):
     return jnp.transpose(column, (0, 2, 1))
 
@@ -454,7 +470,7 @@
     quad = 8 * cap
     hbm = pl.BlockSpec(memory_space=pl.ANY)
     vmem = pl.BlockSpec(memory_space=pltpu.VMEM)
-    return pl.pallas_call(
+    results = pl.pallas_call(
         functools.partial(kernel, sections, holders, cap),
         out_shape=(
             jax.ShapeDtypeStruct(fwd_in.shape, BF16),
@@ -492,6 +508,14 @@
         fwd_in, across(fwd_ids), across(fwd_gates), bwd_in, bwd_grad, across(bwd_ids),
         across(bwd_gates), gate_w, up_w, down_w,
     )
+    return pl.pallas_call(
+        hand_over,
+        out_shape=tuple(jax.ShapeDtypeStruct(r.shape, r.dtype) for r in results),
+        in_specs=[hbm] * 3,
+        out_specs=(hbm,) * 3,
+        scratch_shapes=[pltpu.SemaphoreType.DMA((12,))],
+        name="hand_over",
+    )(*results)
 
 
 def solution(mesh):

time: 225 us -> 333 us (1.48)
  Pallas kernels: 220 us -> 333 us
  local copies, waits for them, and re-layouts: 4.47 us -> 0 us
    pallas_call x0 -> x1, Pallas kernels: none -> 112 us  [per_device(): pl.pallas_call(hand_over, out_shape=tuple((jax.ShapeDtypeStruct(r.shape,...]
    unnamed x7 -> x0, local copies, waits for them, and re-layouts: 4.47 us -> none
where the time goes in v3:
time: 333 us
  Pallas kernels  333 us (100%)
    pallas_call x1, Pallas kernels, per_device(): pl.pallas_call(functools.partial(kernel, sections, holders, cap), out_sha...  220 us
    pallas_call x1, Pallas kernels, per_device(): pl.pallas_call(hand_over, out_shape=tuple((jax.ShapeDtypeStruct(r.shape,...  112 us

profile of v3, /device:TPU:33, one launch (start us, length us, event | category | flops | bytes accessed | tf_op | source)
XLA Modules:
  0.0 333.3 jit_solution(466087750752278761)
XLA Ops:
  0.6 220.2 %routed_layer.1 = (bf16[1,128,3584]{2,1,0:T(8,128)(2,1)}, bf16[1,128,3584]{2,1,0:T(8,128)(2,1)}, bf16[1,1792,512]{2,1,0:T(8,128)(2,1)}) custom-call(bf16[1,128,3584]{2,1,0:T(8,128)(2,1)} %fwd_in.1, s32[1,1,128]{2,1,0:T(1,128)} %bitcast.4, f32[1,1,128]{2,1,0:T(1,128)} %bitcast.5, bf16[1,128,3584]{2,1,0:T(8,128)(2,1)} %bwd_in.1, ...), custom_call_target="tpu_custom_call" | custom-call | tf_op jit(solution)/shard_map/routed_layer/pallas_call | solution.py:473
  220.9 112.4 %hand_over.1 = (bf16[1,128,3584]{2,1,0:T(8,128)(2,1)}, bf16[1,128,3584]{2,1,0:T(8,128)(2,1)}, bf16[1,1792,512]{2,1,0:T(8,128)(2,1)}) custom-call(bf16[1,128,3584]{2,1,0:T(8,128)(2,1)} %get-tuple-element.6.refs_0_, bf16[1,128,3584]{2,1,0:T(8,128)(2,1)} %get-tuple-element.7.refs_1_, bf16[1,1792,512]{2,1,0:T(8,128)(2,1)} %get-tuple-element.8.refs_2_), custom_call_target="tpu_custom_call" | custom-call | tf_op jit(solution)/shard_map/hand_over/pallas_call | solution.py:511
